TPU v7x, 256 devices: a whole 4x4x8 slice. The times are simulated.
256 devices in a mesh: inst: 32 (over x, z_hi, core), tp: 8 (over z_lo, y).
Axes of the slice: x: 4, y: 4, z: 8 (z_hi: 4, z_lo: 2; z = z_hi * 2 + z_lo), core: 2. Of those that a mesh axis runs over, the one named last changes fastest.
Arguments:
- new_states: bfloat16 [3, 1024, 4096], P(None, 'inst'), may hold values from -6 to 6
- attn_gain: bfloat16 [4096], replicated, may hold values from 0.099609375 to 1.8984375
- q_weight: bfloat16 [4096, 4096], P(None, 'tp'), may hold values from -0.09375 to 0.09375
- k_weight: bfloat16 [4096, 1024], P(None, 'tp'), may hold values from -0.1875 to 0.1875
- v_weight: bfloat16 [4096, 1024], P(None, 'tp'), may hold values from -0.09375 to 0.09375
- o_weight: bfloat16 [4096, 4096], P('tp'), may hold values from -0.5 to 0.5
- prompt_keys: bfloat16 [32, 2048, 1024], P('inst', None, 'tp'), may hold values from -100 to 100
- prompt_values: bfloat16 [32, 2048, 1024], P('inst', None, 'tp'), may hold values from -6 to 6
- owner_index: int32 [1], replicated, may hold values from 0 to 31
Outputs:
- branch_out: bfloat16 [3, 1024, 4096], P(None, 'inst')
All inputs are finite; a program needn't handle non-finite values.
Results may differ from a plain program's by a relative error of at most 0.019.
The roundings to bfloat16 on the way count: a program that leaves them out, or rounds other values in their place, can miss the bound.
Values may be sent and summed in bfloat16 or wider, within the bound.
No kernel may reach another device: no remote copies, remote signals or barrier semaphores. Data moves between devices by JAX's collectives and lax.ppermute only.
A program may use at most 64 MiB of HBM per device.

v0:
```python
import jax
import jax.numpy as jnp
from jax import lax
from jax.sharding import PartitionSpec as P

HD = 128


epsilon = 1e-05


def spread(x, axis, root):
    mine = lax.axis_index(axis) == root
    return lax.psum(jnp.where(mine, x, jnp.zeros_like(x)), axis)


def rotate(tensor_in, positions):
    half_dim = tensor_in.shape[-1] // 2
    frequency = jnp.exp(-jnp.arange(half_dim).astype(jnp.float32) * (jnp.log(500000.0) / half_dim))
    angles = positions * frequency
    cosine = jnp.cos(angles)
    sine_part = jnp.sin(angles)
    first_half = tensor_in[..., :half_dim]
    second_half = tensor_in[..., half_dim:]
    return jnp.concatenate(
        [
            first_half * cosine - second_half * sine_part,
            second_half * cosine + first_half * sine_part,
        ],
        axis=-1,
    )


def project(new_states, attn_gain, q_weight, k_weight, v_weight, prompt_len):
    states = new_states.astype(jnp.float32)
    inv_norm = lax.rsqrt(jnp.mean(states * states, axis=-1, keepdims=True) + epsilon)
    normed = (states * inv_norm * attn_gain.astype(jnp.float32)).astype(jnp.bfloat16)
    step_count, samples, feature_dim = normed.shape
    flat_rows = normed.reshape(step_count * samples, feature_dim)
    queries = jnp.dot(flat_rows, q_weight, preferred_element_type=jnp.float32).reshape(
        step_count, samples, -1, HD
    )
    new_keys = jnp.dot(flat_rows, k_weight, preferred_element_type=jnp.float32).reshape(
        step_count, samples, HD
    )
    new_values = jnp.dot(flat_rows, v_weight, preferred_element_type=jnp.float32).reshape(
        step_count, samples, HD
    )
    positions = (prompt_len + jnp.arange(step_count)).astype(jnp.float32)
    queries = rotate(queries, positions.reshape(step_count, 1, 1, 1)).astype(jnp.bfloat16)
    new_keys = rotate(new_keys, positions.reshape(step_count, 1, 1)).astype(jnp.bfloat16)
    return (queries, new_keys, new_values.astype(jnp.bfloat16))


def prompt_part(query_rows, cache_keys, cache_values):
    head_dim = query_rows.shape[-1]
    scores = lax.dot_general(
        query_rows, cache_keys, (((1,), (1,)), ((), ())), preferred_element_type=jnp.float32
    ) * head_dim ** (-0.5)
    row_max = jnp.max(scores, axis=1)
    raw_weights = jnp.exp(scores - row_max[:, None])
    row_sum = jnp.sum(raw_weights, axis=1)
    weighted = jnp.dot(
        raw_weights.astype(jnp.bfloat16), cache_values, preferred_element_type=jnp.float32
    )
    return (row_max, row_sum, weighted)


def finish(queries, new_keys, new_values, row_max, row_sum, weighted):
    head_dim = queries.shape[-1]
    step_count = queries.shape[0]
    own_scores = jnp.einsum(
        "tnqd,und->tnqu", queries, new_keys, preferred_element_type=jnp.float32
    ) * head_dim ** (-0.5)
    step_ids = jnp.arange(step_count)
    causal = (step_ids[None, :] <= step_ids[:, None])[:, None, None, :]
    own_scores = jnp.where(causal, own_scores, -1e30)
    joint_max = jnp.maximum(row_max, jnp.max(own_scores, axis=-1))
    raw_weights = jnp.where(causal, jnp.exp(own_scores - joint_max[..., None]), 0.0)
    rescale = jnp.exp(row_max - joint_max)
    denominator = row_sum * rescale + jnp.sum(raw_weights, axis=-1)
    numerator = weighted * rescale[..., None] + jnp.einsum(
        "tnqu,und->tnqd",
        raw_weights.astype(jnp.bfloat16),
        new_values,
        preferred_element_type=jnp.float32,
    )
    return (numerator / denominator[..., None]).astype(jnp.bfloat16)


def on_device(
    new_states,
    attn_gain,
    q_weight,
    k_weight,
    v_weight,
    o_weight,
    prompt_keys,
    prompt_values,
    owner_index,
):
    prompt_len = prompt_keys.shape[1]
    queries, new_keys, new_values = project(
        new_states, attn_gain, q_weight, k_weight, v_weight, prompt_len
    )
    step_count, samples, head_count, head_dim = queries.shape
    local_keys = prompt_keys[0]
    local_values = prompt_values[0]
    root_index = owner_index[0]
    cache_keys, cache_values = (
        spread(local_keys, "inst", root_index),
        spread(local_values, "inst", root_index),
    )
    step_parts = [
        prompt_part(queries[step_index].reshape(-1, head_dim), cache_keys, cache_values)
        for step_index in range(step_count)
    ]
    row_max = jnp.concatenate([piece[0] for piece in step_parts], axis=0)
    row_sum = jnp.concatenate([piece[1] for piece in step_parts], axis=0)
    weighted = jnp.concatenate([piece[2] for piece in step_parts], axis=0)
    query_shape = (step_count, samples, head_count)
    attended = finish(
        queries,
        new_keys,
        new_values,
        row_max.reshape(query_shape),
        row_sum.reshape(query_shape),
        weighted.reshape(query_shape + (head_dim,)),
    )
    partial_value = jnp.dot(
        attended.reshape(step_count * samples, head_count * head_dim),
        o_weight,
        preferred_element_type=jnp.float32,
    )
    summed = lax.psum(partial_value.astype(jnp.bfloat16), "tp")
    return summed.reshape(step_count, samples, o_weight.shape[1])


def solution(mesh):
    placed = (
        P(None, "inst", None),
        P(),
        P(None, "tp"),
        P(None, "tp"),
        P(None, "tp"),
        P("tp", None),
        P("inst", None, "tp"),
        P("inst", None, "tp"),
        P(),
    )
    return jax.shard_map(
        on_device, mesh=mesh, in_specs=placed, out_specs=P(None, "inst", None), check_vma=False
    )
```

profile of v0, /device:TPU:32, one launch (start us, length us, event | category | flops | bytes accessed | tf_op | source)
XLA Modules:
  0.0 398.6 jit_solution(10927918011547499788)
XLA Ops:
  6.5 0.0 copy-start
  6.5 0.0 all-reduce.6.cloned.1.call-start
  7.3 0.0 copy-start.5
  7.3 0.0 copy-start.4
  7.3 1.1 select_bitcast_fusion
  8.4 0.0 all-reduce.6.cloned.1.call-update
  8.4 0.0 all-reduce.4.cloned.1.call-start
  8.5 0.0 copy-done.5
  8.5 0.3 copy-done.4
  8.8 0.2 fusion
  9.0 6.4 %copy.113 = bf16[512,4096]{1,0:T(8,128)(2,1)} copy(bf16[512,4096]{0,1:T(8,128)(2,1)} %bitcast.69) | data formatting | bytes 8388608 | tf_op jit(solution)/shard_map/dot_general | solution.py:40
  15.4 3.6 fusion.13
  19.1 0.0 copy-done
  19.1 0.4 fusion.5
  19.5 0.1 multiply_cosine_fusion
  19.6 0.1 subtract_convert_fusion
  19.8 0.1 subtract_convert_fusion.1
  19.8 0.1 maximum_bitcast_fusion
  19.9 0.1 pad_maximum_fusion.2
  20.0 0.7 fusion.31
  20.8 0.1 copy.96
  20.9 0.1 fusion.41
  21.0 0.1 copy.118
  21.1 0.1 fusion.35
  21.3 1.7 fusion.3
  23.0 274.9 %all-reduce.6.cloned.1.call-done = (bf16[2048,128]{1,0:T(8,128)(2,1)}, bf16[2048,128]{1,0:T(8,128)(2,1)}) async-done(((bf16[2048,128]{1,0:T(8,128)(2,1)}, bf16[2048,128]{1,0:T(8,128)(2,1)}), (bf16[2048,128]{1,0:T(8,128)(2,1)}, bf16[2048,128]{1,0:T(8,128)(2,1)})) %all-reduce.6.cloned.1.call-update) | async-done | bytes 1048592 | tf_op jit(solution)/shard_map/psum | solution.py:14
  297.8 1.4 fusion.46
  299.3 0.1 concatenate.52
  299.4 1.4 fusion.45
  300.8 0.1 concatenate.53
  300.9 0.0 copy-start.1
  300.9 0.3 fusion.7
  301.2 0.3 fusion.9
  301.5 0.4 copy-done.1
  302.0 0.0 copy-start.3
  302.0 0.4 fusion.19
  302.3 0.4 fusion.17
  302.7 0.0 copy-start.2
  302.7 0.3 copy-done.3
  303.0 0.4 fusion.44
  303.4 0.1 concatenate.54
  303.5 0.3 fusion.11
  303.8 0.0 copy-done.2
  303.8 0.4 fusion.15
  304.2 0.1 fusion.34
  304.2 0.1 copy.100
  304.3 0.1 fusion.42
  304.4 0.1 copy.119
  304.6 0.1 concatenate.57
  304.7 0.1 concatenate.58
  304.8 0.1 concatenate.59
  304.9 0.1 fusion.33
  305.0 0.1 copy.108
  305.1 0.1 copy.98
  305.2 0.2 copy.102
  305.4 0.2 fusion.38
  305.7 0.2 fusion.28
  305.8 0.1 copy.109
  305.9 3.9 convolution_convert_fusion
  309.8 0.0 all-reduce.4.cloned.1.call-update
  309.8 79.9 %all-reduce.4.cloned.1.call-done = bf16[3,32,4096]{2,1,0:T(8,128)(2,1)} async-done(((bf16[3,32,4096]{2,1,0:T(8,128)(2,1)}), bf16[3,32,4096]{2,1,0:T(8,128)(2,1)}) %all-reduce.4.cloned.1.call-update) | async-done | bytes 786448 | tf_op jit(solution)/shard_map/psum | solution.py:135
  389.7 2.1 copy.139
  (9 shorter events, 0.1 us)
Async XLA Ops:
  6.5 12.5 %copy-start = (bf16[4096,128]{1,0:T(8,128)(2,1)S(1)}, bf16[4096,128]{1,0:T(8,128)(2,1)}, u32[]{:S(2)}) copy-start(bf16[4096,128]{1,0:T(8,128)(2,1)} %param.12) | copy-start | bytes 3145732
  6.5 291.3 %all-reduce.6.cloned.1.call-start = ((), (), s32[]{:S(2)}) async-start(), calls=%async_computation.1 | async-start | bytes 2097152 | tf_op jit(solution)/shard_map/psum | solution.py:14
  7.3 1.2 copy-start.5
  7.3 1.5 copy-start.4
  8.4 381.3 %all-reduce.4.cloned.1.call-start = ((), (), s32[]{:S(2)}) async-start(), calls=%async_computation | async-start | bytes 1572864 | tf_op jit(solution)/shard_map/psum | solution.py:135
  300.9 1.0 copy-start.1
  302.0 1.0 copy-start.3
  302.7 1.1 copy-start.2
Sparse Core Ops, SparseCore 0:
  10.0 287.7 all-reduce.5
  309.9 79.7 all-reduce.3
where the time goes:
time: 401 us; the launch traced here: 399 us
  waiting for transfers between devices  355 us (89%)
  matrix products  14.8 us (4%)
  between operations  14.4 us (4%)
  local copies, waits for them, and re-layouts  11 us (3%)
    psum x1, waiting for transfers between devices, spread(): return lax.psum(jnp.where(mine, x, jnp.zeros_like(x)), axis)  275 us
    psum x1, waiting for transfers between devices, on_device(): summed = lax.psum(partial_value.astype(jnp.bfloat16), 'tp')  79.9 us
  transfers between devices with their start and end apart: 2, of which 2 were waited for; matrix products, arithmetic and copies ran while one was open for 4% of the time, Pallas kernels for 0%

commit v1 on v0

--- a/solution.py
+++ b/solution.py
@@ -9,9 +9,68 @@
 epsilon = 1e-05
 
 
-def spread(x, axis, root):
-    mine = lax.axis_index(axis) == root
-    return lax.psum(jnp.where(mine, x, jnp.zeros_like(x)), axis)
+AXES = ("inst", "tp")
+N_X, N_ZH, N_CORE = 4, 4, 2
+
+
+def moves(tp_size, dx=0, dzh=0, dcore=0):
+    pairs = []
+    for x in range(N_X):
+        for zh in range(N_ZH):
+            for core in range(N_CORE):
+                source = (x * N_ZH + zh) * N_CORE + core
+                target = ((x + dx) % N_X * N_ZH + (zh + dzh) % N_ZH) * N_CORE + (core + dcore) % N_CORE
+                pairs += [(source * tp_size + t, target * tp_size + t) for t in range(tp_size)]
+    return pairs
+
+
+def send(block, **delta):
+    return lax.ppermute(block, AXES, moves(lax.axis_size("tp"), **delta))
+
+
+def pick(pieces, index):
+    chosen = pieces[0]
+    for at in range(1, len(pieces)):
+        chosen = jnp.where(index == at, pieces[at], chosen)
+    return chosen
+
+
+def spread(keys, values, root):
+    me = lax.axis_index("inst")
+    core, zh, x = me % N_CORE, me // N_CORE % N_ZH, me // (N_CORE * N_ZH)
+    root_core, root_zh, root_x = root % N_CORE, root // N_CORE % N_ZH, root // (N_CORE * N_ZH)
+    half = keys.shape[0] // 2
+    quarter = half // N_X
+
+    def part(start, size):
+        return jnp.stack(
+            [lax.dynamic_slice_in_dim(a, start, size, 0) for a in (keys, values)]
+        )
+
+    other = send(part((1 - core) * half, half), dcore=1)
+    held = jnp.where(core == root_core, part(core * half, half), other)
+
+    def slab(dx):
+        return lax.dynamic_slice_in_dim(held, (x + dx) % N_X * quarter, quarter, 1)
+
+    got = [slab(0)] + [send(slab(dx), dx=dx) for dx in range(1, N_X)]
+    mine = pick(got, (x - root_x) % N_X)
+    got = [mine] + [send(mine, dzh=dzh) for dzh in range(1, N_ZH)]
+    mine = pick(got, (zh - root_zh) % N_ZH)
+    row = jnp.concatenate([mine] + [send(mine, dx=dx) for dx in range(1, N_X)], axis=1)
+    both = jnp.concatenate([row, send(row, dcore=1)], axis=1)
+    return both[0], both[1]
+
+
+def add_up(partial_value):
+    ranks = lax.axis_size("tp")
+    rows, features = partial_value.shape
+    blocks = partial_value.reshape(rows, ranks, features // ranks).transpose(1, 0, 2)
+    terms = lax.all_to_all(blocks, "tp", 0, 0)
+    summed = jnp.sum(terms.astype(jnp.float32), axis=0).astype(jnp.bfloat16)
+    copies = jnp.broadcast_to(summed, blocks.shape)
+    gathered = lax.all_to_all(copies, "tp", 0, 0)
+    return gathered.transpose(1, 0, 2).reshape(rows, features)
 
 
 def rotate(tensor_in, positions):
@@ -107,10 +166,7 @@
     local_keys = prompt_keys[0]
     local_values = prompt_values[0]
     root_index = owner_index[0]
-    cache_keys, cache_values = (
-        spread(local_keys, "inst", root_index),
-        spread(local_values, "inst", root_index),
-    )
+    cache_keys, cache_values = spread(local_keys, local_values, root_index)
     step_parts = [
         prompt_part(queries[step_index].reshape(-1, head_dim), cache_keys, cache_values)
         for step_index in range(step_count)
@@ -132,7 +188,7 @@
         o_weight,
         preferred_element_type=jnp.float32,
     )
-    summed = lax.psum(partial_value.astype(jnp.bfloat16), "tp")
+    summed = add_up(partial_value.astype(jnp.bfloat16))
     return summed.reshape(step_count, samples, o_weight.shape[1])
 
 

time: 401 us -> 107 us (0.27)
  waiting for transfers between devices: 355 us -> 23.5 us
  blocking collectives: 0 us -> 33.5 us
  starting transfers between devices: 0.04 us -> 17.5 us
  between operations: 14.4 us -> 1.21 us
    psum x2 -> x0, waiting for transfers between devices: 355 us -> none  [the longest x1 275 us: spread(): return lax.psum(jnp.where(mine, x, jnp.zeros_like(x)), axis)]
    all_to_all x0 -> x2, blocking collectives: none -> 33.5 us  [the longest x1 17.8 us: add_up(): terms = lax.all_to_all(blocks, 'tp', 0, 0)]
    ppermute x0 -> x11, waiting for transfers between devices: none -> 23.5 us  [send(): return lax.ppermute(block, AXES, moves(lax.axis_size('tp'), **delta))]
    ppermute x0 -> x11, starting transfers between devices: none -> 17.5 us  [send(): return lax.ppermute(block, AXES, moves(lax.axis_size('tp'), **delta))]
  transfers between devices with their start and end apart: 2 -> 11, of which waited for: 2 -> 8; matrix products, arithmetic and copies ran while one was open for 4% -> 15% of each run, Pallas kernels for 0% -> 0%
where the time goes in v1:
time: 107 us; the launch traced here: 106 us
  blocking collectives  33.5 us (31%)
  waiting for transfers between devices  23.5 us (22%)
  starting transfers between devices  17.5 us (16%)
  local copies, waits for them, and re-layouts  12.8 us (12%)
  matrix products  11.9 us (11%)
  other arithmetic  5.19 us (5%)
  between operations  1.21 us (1%)
    ppermute x11, waiting for transfers between devices, send(): return lax.ppermute(block, AXES, moves(lax.axis_size('tp'), **delta))  23.5 us
    all_to_all x1, blocking collectives, add_up(): terms = lax.all_to_all(blocks, 'tp', 0, 0)  17.8 us
    ppermute x11, starting transfers between devices, send(): return lax.ppermute(block, AXES, moves(lax.axis_size('tp'), **delta))  17.5 us
    all_to_all x1, blocking collectives, add_up(): gathered = lax.all_to_all(copies, 'tp', 0, 0)  15.7 us
    dot_general x1, local copies, waits for them, and re-layouts, project(): jnp.dot(flat_rows, q_weight, preferred_element_type=jnp.float32)  6.47 us
    dot_general x1, matrix products, project(): jnp.dot(flat_rows, q_weight, preferred_element_type=jnp.float32)  3.63 us
    dot_general x1, matrix products, on_device(): jnp.dot(attended.reshape(step_count * samples, head_count * head_dim), o_...  2.99 us
  transfers between devices with their start and end apart: 11, of which 8 were waited for; matrix products, arithmetic and copies ran while one was open for 15% of the time, Pallas kernels for 0%

profile of v1, /device:TPU:32, one launch (start us, length us, event | category | flops | bytes accessed | tf_op | source)
XLA Modules:
  0.0 105.6 jit_solution(14135095829444714553)
XLA Ops:
  0.0 1.3 %constant_dynamic-slice_fusion.5 = (bf16[1,1024,128]{2,1,0:T(8,128)(2,1)S(1)}, bf16[1,1024,128]{2,1,0:T(8,128)(2,1)S(1)}, bf16[1,1024,128]{2,1,0:T(8,128)(2,1)S(1)}, bf16[1,1024,128]{2,1,0:T(8,128)(2,1)S(1)}) fusion(bf16[1,2048,128]{2,1,0:T(8,128)(2,1)} %param.16, s32[]{:T(128)S(6)} %select_n.142, s32[]{:T(128)S(6)} %select_n.143, ...), kind=kLoop, calls=%fused_computation.89 | loop fusion | bytes 2097160 | tf_op jit(solution)/shard_map/dynamic_slice | solution.py:47
  1.4 0.8 pad_maximum_fusion
  2.2 6.5 %copy.141 = bf16[512,4096]{1,0:T(8,128)(2,1)} copy(bf16[512,4096]{0,1:T(8,128)(2,1)} %bitcast.85) | data formatting | bytes 8388608 | tf_op jit(solution)/shard_map/dot_general | solution.py:99
  8.7 0.2 fusion
  9.0 3.6 %fusion.13 = f32[3,32,4,128]{3,1,2,0:T(8,128)S(1)} fusion(bf16[4,128,4096,1]{2,1,0,3:T(8,128)(2,1)} %bitcast.86, bf16[3,32,4096]{2,1,0:T(8,128)(2,1)S(1)} %copy-done.1, f32[4096]{0:T(1024)S(1)} %convert_element_type.86, f32[3,32]{1,0:T(4,128)S(1)} %add_rsqrt_fusion), kind=kOutput, calls=%fused_computation.24 | convolution fusion | flops 404226048 | bytes 5194112 | tf_op jit(solution)/shard_map/dot_general | solution.py:99
  12.6 0.4 fusion.5
  13.1 0.1 multiply_cosine_fusion
  14.0 0.1 subtract_convert_fusion
  14.3 2.8 %collective-permute-start.1 = (bf16[2,256,128]{2,1,0:T(8,128)(2,1)S(1)}, bf16[2,256,128]{2,1,0:T(8,128)(2,1)S(1)}, u32[]{:S(2)}, u32[]{:S(2)}) collective-permute-start(bf16[2,256,128]{2,1,0:T(8,128)(2,1)S(1)} %get-tuple-element.11), channel_id=1, source_target_pairs={{0,192},{1,193},{2,194},{3,195},{4,196},{5,197},{6,198},{7,199},{8... | collective-permute-start | bytes 393224 | tf_op jit(solution)/shard_map/ppermute | solution.py:28
  17.1 0.8 collective-permute-start.2
  17.9 0.9 collective-permute-start.3
  18.9 0.1 pad_maximum_fusion.4
  19.0 4.2 %collective-permute-done.1 = bf16[2,256,128]{2,1,0:T(8,128)(2,1)S(1)} collective-permute-done((bf16[2,256,128]{2,1,0:T(8,128)(2,1)S(1)}, bf16[2,256,128]{2,1,0:T(8,128)(2,1)S(1)}, u32[]{:S(2)}, u32[]{:S(2)}) %collective-permute-start.1) | collective-permute-done | bytes 131104 | tf_op jit(solution)/shard_map/ppermute | solution.py:28
  23.2 1.6 %collective-permute-done.2 = bf16[2,256,128]{2,1,0:T(8,128)(2,1)S(1)} collective-permute-done((bf16[2,256,128]{2,1,0:T(8,128)(2,1)S(1)}, bf16[2,256,128]{2,1,0:T(8,128)(2,1)S(1)}, u32[]{:S(2)}, u32[]{:S(2)}) %collective-permute-start.2) | collective-permute-done | bytes 131104 | tf_op jit(solution)/shard_map/ppermute | solution.py:28
  24.8 3.0 %collective-permute-done.3 = bf16[2,256,128]{2,1,0:T(8,128)(2,1)S(1)} collective-permute-done((bf16[2,256,128]{2,1,0:T(8,128)(2,1)S(1)}, bf16[2,256,128]{2,1,0:T(8,128)(2,1)S(1)}, u32[]{:S(2)}, u32[]{:S(2)}) %collective-permute-start.3) | collective-permute-done | bytes 131104 | tf_op jit(solution)/shard_map/ppermute | solution.py:28
  27.9 5.5 %collective-permute-start.4 = (bf16[2,256,128]{2,1,0:T(8,128)(2,1)S(1)}, bf16[2,256,128]{2,1,0:T(8,128)(2,1)S(1)}, u32[]{:S(2)}, u32[]{:S(2)}) collective-permute-start(bf16[2,256,128]{2,1,0:T(8,128)(2,1)S(1)} %select_select_fusion.1), channel_id=1, source_target_pairs={{0,48},{1,49},{2,50},{3,51},{4,52},{5,53},{6,54},{7,55},{8,56},{9,... | collective-permute-start | bytes 393224 | tf_op jit(solution)/shard_map/ppermute | solution.py:28
  33.4 1.4 %collective-permute-start.5 = (bf16[2,256,128]{2,1,0:T(8,128)(2,1)S(1)}, bf16[2,256,128]{2,1,0:T(8,128)(2,1)S(1)}, u32[]{:S(2)}, u32[]{:S(2)}) collective-permute-start(bf16[2,256,128]{2,1,0:T(8,128)(2,1)S(1)} %select_select_fusion.1), channel_id=1, source_target_pairs={{0,32},{1,33},{2,34},{3,35},{4,36},{5,37},{6,38},{7,39},{8,40},{9,... | collective-permute-start | bytes 393224 | tf_op jit(solution)/shard_map/ppermute | solution.py:28
  34.8 2.4 %collective-permute-start.6 = (bf16[2,256,128]{2,1,0:T(8,128)(2,1)S(1)}, bf16[2,256,128]{2,1,0:T(8,128)(2,1)}, u32[]{:S(2)}, u32[]{:S(2)}) collective-permute-start(bf16[2,256,128]{2,1,0:T(8,128)(2,1)S(1)} %select_select_fusion.1), channel_id=1, source_target_pairs={{0,16},{1,17},{2,18},{3,19},{4,20},{5,21},{6,22},{7,23},{8,24},{9,... | collective-permute-start | bytes 393224 | tf_op jit(solution)/shard_map/ppermute | solution.py:28
  37.2 0.7 fusion.31
  38.0 0.1 copy.122
  38.1 1.5 %collective-permute-done.4 = bf16[2,256,128]{2,1,0:T(8,128)(2,1)S(1)} collective-permute-done((bf16[2,256,128]{2,1,0:T(8,128)(2,1)S(1)}, bf16[2,256,128]{2,1,0:T(8,128)(2,1)S(1)}, u32[]{:S(2)}, u32[]{:S(2)}) %collective-permute-start.4) | collective-permute-done | bytes 131104 | tf_op jit(solution)/shard_map/ppermute | solution.py:28
  39.6 7.5 %collective-permute-done.5 = bf16[2,256,128]{2,1,0:T(8,128)(2,1)S(1)} collective-permute-done((bf16[2,256,128]{2,1,0:T(8,128)(2,1)S(1)}, bf16[2,256,128]{2,1,0:T(8,128)(2,1)S(1)}, u32[]{:S(2)}, u32[]{:S(2)}) %collective-permute-start.5) | collective-permute-done | bytes 131104 | tf_op jit(solution)/shard_map/ppermute | solution.py:28
  47.0 0.6 collective-permute-done.6
  47.6 0.7 constant_dynamic-update-slice_fusion.4
  48.4 1.8 %collective-permute-start.8 = (bf16[2,256,128]{2,1,0:T(8,128)(2,1)}, bf16[2,256,128]{2,1,0:T(8,128)(2,1)S(1)}, u32[]{:S(2)}, u32[]{:S(2)}) collective-permute-start(bf16[2,256,128]{2,1,0:T(8,128)(2,1)} %get-tuple-element.8), channel_id=1, source_target_pairs={{0,128},{1,129},{2,130},{3,131},{4,132},{5,133},{6,134},{7,135},{8... | collective-permute-start | bytes 393224 | tf_op jit(solution)/shard_map/ppermute | solution.py:28
  50.1 1.6 %collective-permute-start.9 = (bf16[2,256,128]{2,1,0:T(8,128)(2,1)}, bf16[2,256,128]{2,1,0:T(8,128)(2,1)}, u32[]{:S(2)}, u32[]{:S(2)}) collective-permute-start(bf16[2,256,128]{2,1,0:T(8,128)(2,1)} %get-tuple-element.8), channel_id=1, source_target_pairs={{0,192},{1,193},{2,194},{3,195},{4,196},{5,197},{6,198},{7,199},{8... | collective-permute-start | bytes 393224 | tf_op jit(solution)/shard_map/ppermute | solution.py:28
  51.9 0.1 copy.146
  52.0 0.1 fusion.35
  52.1 0.6 copy.115
  52.8 4.4 %collective-permute-done.7 = bf16[2,256,128]{2,1,0:T(8,128)(2,1)S(1)} collective-permute-done((bf16[2,256,128]{2,1,0:T(8,128)(2,1)}, bf16[2,256,128]{2,1,0:T(8,128)(2,1)S(1)}, u32[]{:S(2)}, u32[]{:S(2)}) %collective-permute-start.7) | collective-permute-done | bytes 131104 | tf_op jit(solution)/shard_map/ppermute | solution.py:28
  57.2 0.7 collective-permute-done.9
  57.9 1.0 pad_maximum_fusion.1
  58.9 0.3 collective-permute-start.10
  59.2 1.7 %fusion.3 = bf16[3,32,128,1]{2,1,0,3:T(8,128)(2,1)S(1)} fusion(bf16[4096,128]{1,0:T(8,128)(2,1)} %param.13, bf16[3,32,4096]{2,1,0:T(8,128)(2,1)S(1)} %copy-done.1, f32[4096]{0:T(1024)} %copy-done.3, f32[3,32]{1,0:T(4,128)S(1)} %add_rsqrt_fusion), kind=kOutput, calls=%fused_computation.10 | convolution fusion | flops 102248448 | bytes 1876352 | tf_op jit(solution)/shard_map/dot_general | solution.py:105
  61.0 0.9 constant_dynamic-update-slice_fusion.1
  62.0 0.4 fusion.44
  62.4 0.1 concatenate.63
  62.5 0.4 fusion.15
  62.8 0.3 fusion.11
  63.1 0.4 fusion.45
  63.5 0.1 concatenate.62
  63.6 0.4 fusion.17
  64.0 0.3 fusion.9
  64.3 0.4 fusion.46
  64.7 0.1 concatenate.61
  64.8 0.4 fusion.19
  65.2 0.3 fusion.7
  65.5 0.1 copy.126
  65.6 0.1 fusion.42
  65.7 0.2 copy.128
  65.9 0.1 copy.147
  66.0 0.1 concatenate.68
  66.1 0.1 concatenate.67
  66.2 0.1 concatenate.66
  66.3 0.1 fusion.33
  66.6 0.1 copy.124
  66.7 0.2 fusion.38
  66.9 0.2 fusion.28
  67.2 3.0 %convolution_convert_fusion = bf16[96,4096]{1,0:T(8,128)(2,1)S(1)} fusion(bf16[512,4096]{1,0:T(8,128)(2,1)} %param.14, bf16[12,8,4,128]{3,2,1,0:T(4,128)(2,1)S(1)} %bitcast.91), kind=kOutput, calls=%fused_computation | convolution fusion | flops 403046400 | bytes 5079040 | tf_op jit(solution)/shard_map/dot_general | solution.py:186
  70.2 17.8 %all_to_all.10 = bf16[8,96,512]{2,1,0:T(8,128)(2,1)S(1)} all-to-all(bf16[8,96,512]{2,1,0:T(8,128)(2,1)S(1)} %bitcast.88), channel_id=1, replica_groups=mesh['inst'=32,'tp'=8] {'tp'}, dimensions={0} | all-to-all | bytes 1572864 | tf_op jit(solution)/shard_map/all_to_all | solution.py:69
  88.1 0.1 reduce_sum.62
  88.2 15.7 %all_to_all.11 = bf16[8,96,512]{2,1,0:T(8,128)(2,1)S(1)} all-to-all(bf16[8,96,512]{2,1,0:T(8,128)(2,1)S(1)} %broadcast_in_dim.39), channel_id=1, replica_groups=mesh['inst'=32,'tp'=8] {'tp'}, dimensions={0} | all-to-all | bytes 1572864 | tf_op jit(solution)/shard_map/all_to_all | solution.py:72
  103.9 0.4 copy.137
  104.4 1.2 %reshape_reshape.3 = bf16[3,32,4096]{2,1,0:T(8,128)(2,1)} reshape(bf16[96,8,512]{2,1,0:T(8,128)(2,1)S(1)} %copy.137) | data formatting | bytes 1572864 | tf_op jit(solution)/shard_map/reshape;reshape | solution.py:192
  (41 shorter events, 1.0 us)
Async XLA Ops:
  0.0 12.6 %copy-start = (bf16[4096,128]{1,0:T(8,128)(2,1)S(1)}, bf16[4096,128]{1,0:T(8,128)(2,1)}, u32[]{:S(2)}) copy-start(bf16[4096,128]{1,0:T(8,128)(2,1)} %param.12) | copy-start | bytes 3145732
  2.2 12.0 %collective-permute-start = (bf16[2,1024,128]{2,1,0:T(8,128)(2,1)}, bf16[2,1024,128]{2,1,0:T(8,128)(2,1)}, u32[]{:S(2)}, u32[]{:S(2)}) collective-permute-start(bf16[2,1024,128]{2,1,0:T(8,128)(2,1)} %pad_maximum_fusion), channel_id=1, source_target_pairs={{0,8},{1,9},{2,10},{3,11},{4,12},{5,13},{6,14},{7,15},{8,0},{9,1},... | collective-permute-start | bytes 1572872 | tf_op jit(solution)/shard_map/ppermute | solution.py:28
  2.2 6.5 %copy-start.4 = (bf16[4096]{0:T(1024)(128)(2,1)S(1)}, bf16[4096]{0:T(1024)(128)(2,1)}, u32[]{:S(2)}) copy-start(bf16[4096]{0:T(1024)(128)(2,1)} %param.10) | copy-start | bytes 24580
  2.2 6.5 %copy-start.1 = (bf16[3,32,4096]{2,1,0:T(8,128)(2,1)S(1)}, bf16[3,32,4096]{2,1,0:T(8,128)(2,1)}, u32[]{:S(2)}) copy-start(bf16[3,32,4096]{2,1,0:T(8,128)(2,1)} %param.9) | copy-start | bytes 2359300
  8.7 5.2 %copy-start.3 = (f32[4096]{0:T(1024)}, f32[4096]{0:T(1024)S(1)}, u32[]{:S(2)}) copy-start(f32[4096]{0:T(1024)S(1)} %convert_element_type.86) | copy-start | bytes 49156
  14.3 8.9 %collective-permute-start.1 = (bf16[2,256,128]{2,1,0:T(8,128)(2,1)S(1)}, bf16[2,256,128]{2,1,0:T(8,128)(2,1)S(1)}, u32[]{:S(2)}, u32[]{:S(2)}) collective-permute-start(bf16[2,256,128]{2,1,0:T(8,128)(2,1)S(1)} %get-tuple-element.11), channel_id=1, source_target_pairs={{0,192},{1,193},{2,194},{3,195},{4,196},{5,197},{6,198},{7,199},{8... | collective-permute-start | bytes 393224 | tf_op jit(solution)/shard_map/ppermute | solution.py:28
  17.1 7.7 %collective-permute-start.2 = (bf16[2,256,128]{2,1,0:T(8,128)(2,1)S(1)}, bf16[2,256,128]{2,1,0:T(8,128)(2,1)S(1)}, u32[]{:S(2)}, u32[]{:S(2)}) collective-permute-start(bf16[2,256,128]{2,1,0:T(8,128)(2,1)S(1)} %get-tuple-element.10), channel_id=1, source_target_pairs={{0,128},{1,129},{2,130},{3,131},{4,132},{5,133},{6,134},{7,135},{8... | collective-permute-start | bytes 393224 | tf_op jit(solution)/shard_map/ppermute | solution.py:28
  17.9 9.9 %collective-permute-start.3 = (bf16[2,256,128]{2,1,0:T(8,128)(2,1)S(1)}, bf16[2,256,128]{2,1,0:T(8,128)(2,1)S(1)}, u32[]{:S(2)}, u32[]{:S(2)}) collective-permute-start(bf16[2,256,128]{2,1,0:T(8,128)(2,1)S(1)} %get-tuple-element.9), channel_id=1, source_target_pairs={{0,64},{1,65},{2,66},{3,67},{4,68},{5,69},{6,70},{7,71},{8,72},{9,... | collective-permute-start | bytes 393224 | tf_op jit(solution)/shard_map/ppermute | solution.py:28
  27.9 11.7 %collective-permute-start.4 = (bf16[2,256,128]{2,1,0:T(8,128)(2,1)S(1)}, bf16[2,256,128]{2,1,0:T(8,128)(2,1)S(1)}, u32[]{:S(2)}, u32[]{:S(2)}) collective-permute-start(bf16[2,256,128]{2,1,0:T(8,128)(2,1)S(1)} %select_select_fusion.1), channel_id=1, source_target_pairs={{0,48},{1,49},{2,50},{3,51},{4,52},{5,53},{6,54},{7,55},{8,56},{9,... | collective-permute-start | bytes 393224 | tf_op jit(solution)/shard_map/ppermute | solution.py:28
  33.4 13.6 %collective-permute-start.5 = (bf16[2,256,128]{2,1,0:T(8,128)(2,1)S(1)}, bf16[2,256,128]{2,1,0:T(8,128)(2,1)S(1)}, u32[]{:S(2)}, u32[]{:S(2)}) collective-permute-start(bf16[2,256,128]{2,1,0:T(8,128)(2,1)S(1)} %select_select_fusion.1), channel_id=1, source_target_pairs={{0,32},{1,33},{2,34},{3,35},{4,36},{5,37},{6,38},{7,39},{8,40},{9,... | collective-permute-start | bytes 393224 | tf_op jit(solution)/shard_map/ppermute | solution.py:28
  34.8 12.8 %collective-permute-start.6 = (bf16[2,256,128]{2,1,0:T(8,128)(2,1)S(1)}, bf16[2,256,128]{2,1,0:T(8,128)(2,1)}, u32[]{:S(2)}, u32[]{:S(2)}) collective-permute-start(bf16[2,256,128]{2,1,0:T(8,128)(2,1)S(1)} %select_select_fusion.1), channel_id=1, source_target_pairs={{0,16},{1,17},{2,18},{3,19},{4,20},{5,21},{6,22},{7,23},{8,24},{9,... | collective-permute-start | bytes 393224 | tf_op jit(solution)/shard_map/ppermute | solution.py:28
  38.1 13.7 %copy-start.5 = (pred[3,3]{1,0:T(4,128)(4,1)}, pred[3,3]{1,0:T(4,128)(4,1)S(1)}, u32[]{:S(2)}) copy-start(pred[3,3]{1,0:T(4,128)(4,1)S(1)} %iota_compare_fusion) | copy-start | bytes 31
  48.4 8.9 %collective-permute-start.7 = (bf16[2,256,128]{2,1,0:T(8,128)(2,1)}, bf16[2,256,128]{2,1,0:T(8,128)(2,1)S(1)}, u32[]{:S(2)}, u32[]{:S(2)}) collective-permute-start(bf16[2,256,128]{2,1,0:T(8,128)(2,1)} %get-tuple-element.8), channel_id=1, source_target_pairs={{0,64},{1,65},{2,66},{3,67},{4,68},{5,69},{6,70},{7,71},{8,72},{9,... | collective-permute-start | bytes 393224 | tf_op jit(solution)/shard_map/ppermute | solution.py:28
  48.4 8.9 %collective-permute-start.8 = (bf16[2,256,128]{2,1,0:T(8,128)(2,1)}, bf16[2,256,128]{2,1,0:T(8,128)(2,1)S(1)}, u32[]{:S(2)}, u32[]{:S(2)}) collective-permute-start(bf16[2,256,128]{2,1,0:T(8,128)(2,1)} %get-tuple-element.8), channel_id=1, source_target_pairs={{0,128},{1,129},{2,130},{3,131},{4,132},{5,133},{6,134},{7,135},{8... | collective-permute-start | bytes 393224 | tf_op jit(solution)/shard_map/ppermute | solution.py:28
  50.1 7.8 %collective-permute-start.9 = (bf16[2,256,128]{2,1,0:T(8,128)(2,1)}, bf16[2,256,128]{2,1,0:T(8,128)(2,1)}, u32[]{:S(2)}, u32[]{:S(2)}) collective-permute-start(bf16[2,256,128]{2,1,0:T(8,128)(2,1)} %get-tuple-element.8), channel_id=1, source_target_pairs={{0,192},{1,193},{2,194},{3,195},{4,196},{5,197},{6,198},{7,199},{8... | collective-permute-start | bytes 393224 | tf_op jit(solution)/shard_map/ppermute | solution.py:28
  58.9 2.9 %collective-permute-start.10 = (bf16[2,1024,128]{2,1,0:T(8,128)(2,1)S(1)}, bf16[2,1024,128]{2,1,0:T(8,128)(2,1)S(1)}, u32[]{:S(2)}, u32[]{:S(2)}) collective-permute-start(bf16[2,1024,128]{2,1,0:T(8,128)(2,1)S(1)} %pad_maximum_fusion.1), channel_id=1, source_target_pairs={{0,8},{1,9},{2,10},{3,11},{4,12},{5,13},{6,14},{7,15},{8,0},{9,1},... | collective-permute-start | bytes 1572872 | tf_op jit(solution)/shard_map/ppermute | solution.py:28
  62.4 0.8 copy-start.2
  64.7 0.9 copy-start.6
